TPU v7x, 256 devices: a whole 4x4x8 slice. The times are simulated.
256 devices in a mesh: section: 8 (over x, y_lo), tp: 32 (over z, y_hi, core).
Axes of the slice: x: 4, y: 4 (y_hi: 2, y_lo: 2; y = y_hi * 2 + y_lo), z: 8, core: 2. Of those that a mesh axis runs over, the one named last changes fastest.
Arguments:
- resid: bfloat16 [8, 512, 8192], P('section', 'tp'), may hold values from -36 to 36
- pending: bfloat16 [8, 512, 8192], P('section', 'tp'), may hold values from -6 to 6
- doc_ids: int32 [8, 512], P('section'), may hold values from 0 to 3, never falling along the last dimension, each value on 1 to 256 neighbouring positions
- norm_gain: bfloat16 [8, 8192], P('section'), may hold values from 0.25 to 1.75
- q_weight: bfloat16 [8, 8192, 8192], P('section', None, 'tp'), may hold values from -2 to 2
- kv_weight: bfloat16 [8, 8192, 1024], P('section', None, 'tp'), may hold values from -1 to 1
- o_weight: bfloat16 [8, 8192, 8192], P('section', 'tp'), may hold values from -0.25 to 0.25
Outputs:
- next_resid: bfloat16 [8, 512, 8192], P('section', 'tp')
- next_output: bfloat16 [8, 512, 8192], P('section', 'tp')
Inputs may be any that keep to these rules, and one draw needn't show every extreme that they name: `doc_ids`: ids never fall along the tokens of a micro-batch; every document has 1 to 256 tokens, and one has exactly that many.
All inputs are finite; a program needn't handle non-finite values.
Results may differ from a plain program's by a relative error of at most 0.03.
Values may be sent and summed in bfloat16 or wider, within the bound.
A program may use at most 128 MiB of HBM per device.

v0:
```python
import math

import jax
import jax.numpy as jnp
from jax import lax
from jax.sharding import PartitionSpec as P

HEADS = 64
KV_HEADS = 4
HD = 128


def shifted(value, axis, steps):
    count = lax.axis_size(axis)
    pairs = [(source, (source + steps) % count) for source in range(count)]
    return lax.ppermute(value, axis, pairs)


def rms_normed(stream, gain):
    values = stream.astype(jnp.float32)
    mean_square = jnp.mean(values * values, axis=-1, keepdims=True)
    return (values * lax.rsqrt(mean_square + 1e-05) * gain.astype(jnp.float32)).astype(jnp.bfloat16)


def doc_mask(documents):
    order = jnp.arange(documents.shape[0], dtype=jnp.int32)
    return (order[:, None] >= order[None, :]) & (documents[:, None] == documents[None, :])


def attend(query_heads, keys, values, mask):
    scores = jnp.einsum(
        "thd,sd->hts", query_heads, keys, preferred_element_type=jnp.float32
    ) / math.sqrt(keys.shape[1])
    probs = jax.nn.softmax(jnp.where(mask[None], scores, -1e30), axis=-1).astype(jnp.bfloat16)
    context = jnp.einsum("hts,sd->thd", probs, values, preferred_element_type=jnp.float32).astype(
        jnp.bfloat16
    )
    return context.reshape(context.shape[0], context.shape[1] * context.shape[2])


def body(resid, pending, doc_ids, norm_gain, q_weight, kv_weight, o_weight):
    stream = resid[0]
    carried = (stream.astype(jnp.float32) + pending[0].astype(jnp.float32)).astype(jnp.bfloat16)[
        None
    ]
    normed = rms_normed(stream, norm_gain[0])
    w_query = q_weight[0]
    w_keyval = kv_weight[0]
    w_out = o_weight[0]
    query_width = w_query.shape[1]
    piece = lax.all_gather(normed, "tp", axis=0, tiled=True)
    query_part = jnp.dot(piece, w_query, preferred_element_type=jnp.float32).astype(jnp.bfloat16)
    keyval_part = jnp.dot(piece, w_keyval, preferred_element_type=jnp.float32).astype(jnp.bfloat16)
    projected = jnp.concatenate([query_part, keyval_part], axis=1)
    queries = projected[:, :query_width]
    keyvals = lax.all_gather(projected[:, query_width:], "tp", axis=1, tiled=True)
    token_count = queries.shape[0]
    per_block = query_width // HD
    kv_head = lax.axis_index("tp") * per_block // (HEADS // KV_HEADS)
    keys = lax.dynamic_slice_in_dim(keyvals, kv_head * HD, HD, 1)
    values = lax.dynamic_slice_in_dim(keyvals, KV_HEADS * HD + kv_head * HD, HD, 1)
    mask = doc_mask(doc_ids[0])
    context = attend(queries.reshape(token_count, per_block, HD), keys, values, mask)
    row_count = stream.shape[0]
    summed = lax.psum(
        jnp.dot(context, w_out, preferred_element_type=jnp.float32).astype(jnp.bfloat16), "tp"
    ).astype(jnp.float32)
    share = lax.dynamic_slice_in_dim(summed, lax.axis_index("tp") * row_count, row_count, 0)
    module_out = share.astype(jnp.bfloat16)[None]
    next_resid, next_output = shifted((carried, module_out), "section", 1)
    return (next_resid, next_output)


def solution(mesh):
    in_specs = (
        P("section", "tp", None),
        P("section", "tp", None),
        P("section", None),
        P("section", None),
        P("section", None, "tp"),
        P("section", None, "tp"),
        P("section", "tp", None),
    )
    out_specs = (P("section", "tp", None), P("section", "tp", None))
    return jax.shard_map(body, mesh=mesh, in_specs=in_specs, out_specs=out_specs, check_vma=False)
```

profile of v0, /device:TPU:32, one launch (start us, length us, event | category | flops | bytes accessed | tf_op | source)
XLA Modules:
  0.0 512.1 jit_solution(8853235838481877879)
XLA Ops:
  7.2 0.0 all-gather.3.cloned.1.call-start
  7.2 0.8 mul.44
  8.1 1.1 fusion.14
  9.2 1.8 fusion.16
  11.0 0.0 all-gather.5.cloned.1.call-start
  11.1 104.1 %all-gather.3.cloned.1.call-done = bf16[512,8192]{1,0:T(8,128)(2,1)} async-done(((bf16[16,8192]{1,0:T(8,128)(2,1)}), bf16[512,8192]{1,0:T(8,128)(2,1)}) %all-gather.3.cloned.1.call-update) | async-done | bytes 8388624 | tf_op jit(solution)/shard_map/all_gather | solution.py:51
  115.2 6.6 %convolution_convert_fusion.2 = bf16[512,32]{0,1:T(8,128)(2,1)} fusion(bf16[512,8192]{1,0:T(8,128)(2,1)} %all-gather.3.cloned.1.call-done, bf16[1,8192,32]{1,2,0:T(8,128)(2,1)S(1)} %copy-done), kind=kOutput, calls=%fused_computation.11 | convolution fusion | flops 268451840 | bytes 8945664 | tf_op jit(solution)/shard_map/dot_general | solution.py:53
  121.8 0.0 all-reduce.2.cloned.1.call-start
  121.9 0.2 fusion.10
  122.1 6.9 %fusion.5 = bf16[512,256]{0,1:T(8,128)(2,1)S(1)} fusion(bf16[512,8192]{1,0:T(8,128)(2,1)} %all-gather.3.cloned.1.call-done, bf16[1,8192,256]{2,1,0:T(8,128)(2,1)} %param.11), kind=kOutput, calls=%fused_computation.10 | convolution fusion | flops 2147614720 | bytes 12845056 | tf_op jit(solution)/shard_map/dot_general | solution.py:52
  129.1 66.3 %all-gather.5.cloned.1.call-done = bf16[512,1024]{0,1:T(8,128)(2,1)} async-done(((bf16[512,32]{0,1:T(8,128)(2,1)}), bf16[512,1024]{0,1:T(8,128)(2,1)}) %all-gather.5.cloned.1.call-update) | async-done | bytes 1048592 | tf_op jit(solution)/shard_map/all_gather | solution.py:56
  195.3 1.8 fusion.50
  197.2 2.2 convolution_convert_fusion.1
  199.4 7.8 %convolution_convert_fusion = bf16[512,8192]{1,0:T(8,128)(2,1)} fusion(bf16[512,256]{0,1:T(8,128)(2,1)S(1)} %bitcast.64, bf16[1,256,8192]{2,1,0:T(8,128)(2,1)} %param.13), kind=kOutput, calls=%fused_computation.1 | convolution fusion | flops 2151677952 | bytes 12845056 | tf_op jit(solution)/shard_map/dot_general | solution.py:66
  207.2 0.9 copy-done.1
  208.1 0.1 copy-done.2
  208.2 0.1 fusion.17
  208.3 0.6 collective-permute-start
  208.9 285.0 %all-reduce.2.cloned.1.call-done = bf16[512,8192]{1,0:T(8,128)(2,1)} async-done(((bf16[512,8192]{1,0:T(8,128)(2,1)}), bf16[512,8192]{1,0:T(8,128)(2,1)}) %all-reduce.2.cloned.1.call-update) | async-done | bytes 8388624 | tf_op jit(solution)/shard_map/psum | solution.py:65
  493.8 1.0 fusion.19
  494.8 0.8 collective-permute-start.1
  495.6 8.6 %collective-permute-done.1 = bf16[1,16,8192]{2,1,0:T(8,128)(2,1)S(1)} collective-permute-done((bf16[1,16,8192]{2,1,0:T(8,128)(2,1)S(1)}, bf16[1,16,8192]{2,1,0:T(8,128)(2,1)S(1)}, u32[]{:S(2)}, u32[]{:S(2)}) %collective-permute-start.1) | collective-permute-done | bytes 262176 | tf_op jit(solution)/shard_map/ppermute | solution.py:16
  504.1 0.7 copy.19
  504.8 0.7 copy.20
  (11 shorter events, 0.1 us)
Async XLA Ops:
  7.2 108.0 %copy-start = (bf16[1,8192,32]{1,2,0:T(8,128)(2,1)S(1)}, bf16[1,8192,32]{1,2,0:T(8,128)(2,1)}, u32[]{:S(2)}) copy-start(bf16[1,8192,32]{1,2,0:T(8,128)(2,1)} %param.12) | copy-start | bytes 1572868
  7.2 108.0 %all-gather.3.cloned.1.call-start = ((), (), s32[]{:S(2)}) async-start(), calls=%async_computation | async-start | bytes 8650752 | tf_op jit(solution)/shard_map/all_gather | solution.py:51
  11.0 110.9 %copy-start.3 = (s32[1,512]{1,0:T(1,128)S(1)}, s32[1,512]{1,0:T(1,128)}, u32[]{:S(2)}) copy-start(s32[1,512]{1,0:T(1,128)} %param.9) | copy-start | bytes 6148
  11.0 184.3 %all-gather.5.cloned.1.call-start = ((), (), s32[]{:S(2)}) async-start(), calls=%async_computation.1 | async-start | bytes 1081344 | tf_op jit(solution)/shard_map/all_gather | solution.py:56
  121.8 372.0 %all-reduce.2.cloned.1.call-start = ((), (), s32[]{:S(2)}) async-start(), calls=%async_computation.2 | async-start | bytes 16777216 | tf_op jit(solution)/shard_map/psum | solution.py:65
  207.2 0.9 copy-start.1
  207.2 1.0 copy-start.2
  208.3 287.3 %collective-permute-start = (bf16[1,16,8192]{2,1,0:T(8,128)(2,1)S(1)}, bf16[1,16,8192]{2,1,0:T(8,128)(2,1)S(1)}, u32[]{:S(2)}, u32[]{:S(2)}) collective-permute-start(bf16[1,16,8192]{2,1,0:T(8,128)(2,1)S(1)} %fusion.17), channel_id=1, source_target_pairs={{0,32},{32,64},{64,96},{96,128},{128,160},{160,192},{192,224},{224... | collective-permute-start | bytes 786440 | tf_op jit(solution)/shard_map/ppermute | solution.py:16
  494.8 9.3 %collective-permute-start.1 = (bf16[1,16,8192]{2,1,0:T(8,128)(2,1)S(1)}, bf16[1,16,8192]{2,1,0:T(8,128)(2,1)S(1)}, u32[]{:S(2)}, u32[]{:S(2)}) collective-permute-start(bf16[1,16,8192]{2,1,0:T(8,128)(2,1)S(1)} %fusion.19), channel_id=1, source_target_pairs={{0,32},{32,64},{64,96},{96,128},{128,160},{160,192},{192,224},{224... | collective-permute-start | bytes 786440 | tf_op jit(solution)/shard_map/ppermute | solution.py:16
Sparse Core Ops, SparseCore 0:
  11.4 103.7 all-gather.2
  121.9 73.3 all-gather.4
  207.3 286.4 all-reduce.1
where the time goes:
time: 518 us; the launch traced here: 512 us
  waiting for transfers between devices  464 us (90%)
  matrix products  25.4 us (5%)
  between operations  13.8 us (3%)
    psum x1, waiting for transfers between devices, body(): lax.psum(jnp.dot(context, w_out, preferred_element_type=jnp.float32).asty...  285 us
    all_gather x1, waiting for transfers between devices, body(): piece = lax.all_gather(normed, 'tp', axis=0, tiled=True)  104 us
    all_gather x1, waiting for transfers between devices, body(): lax.all_gather(projected[:, query_width:], 'tp', axis=1, tiled=True)  66.3 us
  transfers between devices with their start and end apart: 5, of which 4 were waited for; matrix products, arithmetic and copies ran while one was open for 2% of the time, Pallas kernels for 0%

commit v1 on v0

v1 whole, which is shorter than its diff:
```python
import functools
import math

import jax
import jax.numpy as jnp
from jax import lax
from jax.experimental import pallas as pl
from jax.experimental.pallas import tpu as pltpu
from jax.sharding import PartitionSpec as P

D = 8192
HD = 128
Z = 8
ROWS = 16
TOK = 256
NC = 4
KC = D // NC
AG_OFF = (0, 0, 1, 2)
RS_OFF = (0, 1, 2, 3)
MESH = pl.DeviceIdType.MESH
F32 = jnp.float32
BF16 = jnp.bfloat16
SAME, OTHER = 0, 1
ZP, ZM, YY = 0, 1, 2

YE = {4: 0, 3: 1, -3: 2, 2: 3, -2: 4}
RP = {3: 5, 2: 6, 1: 7, 0: 8}
RM = {-3: 9, -2: 10, -1: 11, 0: 12}
QP = {1: 13, 0: 14}
QM = {-1: 15, 0: 16}
RY = 17
SLOTS = 18


def kernel(
    resid, pending, doc_ids, gain, wq_hbm, wkv_hbm, wo_hbm,
    next_resid, next_output,
    xg, wq, wkv, wo, accq, acckv, kvs, kvr, ctx, part, rsb, carr,
    ag_s, ag_r, rs_s, rs_r, kv_s, kv_r, lw, ws, wr, sh_s, sh_r,
):
    sec = lax.axis_index("section")
    t = lax.axis_index("tp")
    z, yh, c = t // 4, (t // 2) % 2, t % 2

    def at(zz, yy, cc):
        return (sec, (zz * 2 + yy) * 2 + cc)

    neighbour = (
        at((z + 1) % Z, yh, c),
        at((z + Z - 1) % Z, yh, c),
        at(z, 1 - yh, c),
    )
    sibling = at(z, yh, 1 - c)
    next_sec = ((sec + 1) % 8, t)
    prev_sec = ((sec + 7) % 8, t)

    def block(kind, d):
        b = ((z + d + Z) % Z) * 2 + (yh if kind == SAME else 1 - yh)
        return pl.ds(pl.multiple_of(b * ROWS, ROWS), ROWS)

    barrier = pltpu.get_barrier_semaphore()
    for o in range(1, 32):
        pl.semaphore_signal(barrier, inc=1, device_id=(sec, (t + o) % 32), device_id_type=MESH)
    for dev in (next_sec, prev_sec):
        pl.semaphore_signal(barrier, inc=1, device_id=dev, device_id_type=MESH)

    def cols(j):
        return pl.ds(j * KC, KC)

    pieces = [(wkv_hbm, wkv.at[pl.ds(pl.multiple_of(c * 32, 32), 32)])]
    for j in range(NC):
        pieces.append((wq_hbm.at[cols(j)], wq.at[c, cols(j)]))
    for j in range(NC):
        pieces.append(
            (wo_hbm.at[:, cols(j)], wo.at[pl.ds(pl.multiple_of(c * 256, 256), 256), cols(j)])
        )
    local = [pltpu.make_async_copy(s, d, lw.at[i]) for i, (s, d) in enumerate(pieces)]
    far = [
        pltpu.make_async_remote_copy(
            src_ref=s, dst_ref=d, send_sem=ws.at[i], recv_sem=wr.at[i],
            device_id=sibling, device_id_type=MESH,
        )
        for i, (s, d) in enumerate(pieces)
    ]
    for copy in local:
        copy.start()

    stream = resid[...].astype(F32)
    scale = lax.rsqrt(jnp.mean(stream * stream, axis=-1, keepdims=True) + 1e-05)
    for j in range(NC):
        piece = resid[:, j * KC : (j + 1) * KC].astype(F32)
        xg[j, block(SAME, 0)] = (
            piece * scale * gain[:, j * KC : (j + 1) * KC].astype(F32)
        ).astype(BF16)

    pl.semaphore_wait(barrier, 33)

    sends = []

    count = [0] * NC

    def ag_send(j, kind, d, way):
        dd = d - 1 if way == ZP else d + 1 if way == ZM else d
        kk = kind if way != YY else 1 - kind
        ref = xg.at[j, block(kind, d)]
        copy = pltpu.make_async_remote_copy(
            src_ref=ref, dst_ref=ref,
            send_sem=ag_s.at[j * 16 + count[j]], recv_sem=ag_r.at[j * 16 + kk * 8 + dd % 8],
            device_id=neighbour[way], device_id_type=MESH,
        )
        count[j] += 1
        copy.start()
        sends.append(copy)

    def ag_wait(j, kind, d):
        ref = xg.at[j, block(kind, d)]
        pltpu.make_async_remote_copy(
            src_ref=ref, dst_ref=ref,
            send_sem=ag_s.at[j * 16], recv_sem=ag_r.at[j * 16 + kind * 8 + d % 8],
            device_id=neighbour[YY], device_id_type=MESH,
        ).wait_recv()

    def ag_step(j, step):
        even = j % 2 == 0
        if step == 0:
            ag_send(j, SAME, 0, ZP)
            ag_send(j, SAME, 0, ZM)
            ag_send(j, SAME, 0, YY)
        elif step == 1:
            ag_wait(j, SAME, -1)
            ag_send(j, SAME, -1, ZP)
            ag_wait(j, SAME, 1)
            ag_send(j, SAME, 1, ZM)
            ag_wait(j, OTHER, 0)
            ag_send(j, OTHER, 0, ZP)
            ag_send(j, OTHER, 0, ZM)
        elif step == 2:
            ag_wait(j, SAME, -2)
            ag_send(j, SAME, -2, ZP)
            if not even:
                ag_send(j, SAME, -2, YY)
            ag_wait(j, SAME, 2)
            ag_send(j, SAME, 2, ZM)
            if not even:
                ag_send(j, SAME, 2, YY)
            ag_wait(j, OTHER, -1)
            ag_wait(j, OTHER, 1)
            if even:
                ag_send(j, OTHER, -1, ZP)
                ag_send(j, OTHER, 1, ZM)
        elif step == 3:
            ag_wait(j, SAME, -3)
            if even:
                ag_send(j, SAME, -3, ZP)
            ag_send(j, SAME, -3, YY)
            ag_wait(j, SAME, 3)
            if not even:
                ag_send(j, SAME, 3, ZM)
            ag_send(j, SAME, 3, YY)
        elif step == 4:
            ag_wait(j, SAME, 4)
            ag_send(j, SAME, 4, YY)
        elif step == 5:
            for d in (-2, 2, -3, 3, 4):
                ag_wait(j, OTHER, d)

    def weight_ready(i):
        local[i].wait()
        far[i].wait_recv()

    def project_kv(j):
        if j == 0:
            weight_ready(0)
        term = lax.dot_general(
            wkv[:, j * KC : (j + 1) * KC], xg[j], (((1,), (1,)), ((), ())),
            preferred_element_type=F32,
        )
        acckv[...] = term if j == 0 else acckv[...] + term

    def project_q(j):
        weight_ready(1 + j)
        for cc in range(2):
            term = jnp.dot(
                xg[j], wq[cc, j * KC : (j + 1) * KC, :], preferred_element_type=F32
            )
            span = slice(cc * 256, (cc + 1) * 256)
            accq[:, span] = term if j == 0 else accq[:, span] + term

    for r in range(max(AG_OFF) + 6):
        for j in range(NC):
            step = r - AG_OFF[j]
            if 0 <= step <= 5:
                ag_step(j, step)
        if r == 0:
            for copy in far:
                copy.start()
        for j in range(NC - 1):
            if r - AG_OFF[j] == 5:
                project_kv(j)
                project_q(j)

    project_kv(NC - 1)
    kvs[...] = acckv[...].astype(BF16)
    kv_rows = pl.ds(pl.multiple_of((z // 4) * 128 + yh * 64, 64), 64)
    kv_index = (z // 4) * 4 + yh * 2 + c
    kv_copies = []
    for n in range(8):
        zz, yy, cc = 2 * (z % 4) + n // 4, (n // 2) % 2, n % 2
        mine = (zz == z) & (yy == yh) & (cc == c)
        copy = pltpu.make_async_remote_copy(
            src_ref=kvs, dst_ref=kvr.at[c, kv_rows],
            send_sem=kv_s.at[n], recv_sem=kv_r.at[kv_index],
            device_id=at(zz, yy, cc), device_id_type=MESH,
        )
        kv_copies.append((mine, copy))

        @pl.when(mine)
        def _():
            pltpu.make_async_copy(kvs, kvr.at[c, kv_rows], kv_r.at[kv_index]).start()

        @pl.when(jnp.logical_not(mine))
        def _(copy=copy):
            copy.start()

    carr[...] = (resid[...].astype(F32) + pending[...].astype(F32)).astype(BF16)
    carry = pltpu.make_async_remote_copy(
        src_ref=carr, dst_ref=next_resid,
        send_sem=sh_s.at[NC], recv_sem=sh_r.at[NC],
        device_id=next_sec, device_id_type=MESH,
    )
    carry.start()

    project_q(NC - 1)

    docs = doc_ids[...].astype(F32)
    row = lax.broadcasted_iota(jnp.int32, (TOK, 1), 0)
    mine_at = ((row // 16) * 32 + c * 16 + row % 16).astype(F32)
    key = lax.broadcasted_iota(jnp.int32, (1, 2 * TOK), 1)
    key_at = (((key % TOK) // 16) * 32 + (key // TOK) * 16 + key % 16).astype(F32)
    first = jnp.zeros((TOK, 1), F32)
    for k in range(1, 4):
        begin = jnp.sum(jnp.where(docs < k, 1.0, 0.0), axis=-1, keepdims=True)
        first = jnp.maximum(first, jnp.where(mine_at >= begin, begin, 0.0))
    mask = (key_at <= mine_at) & (key_at >= first)

    for i in range(8):
        ref = kvr.at[i % 2, pl.ds((i // 2) * 64, 64)]
        pltpu.make_async_remote_copy(
            src_ref=ref, dst_ref=ref, send_sem=kv_s.at[0], recv_sem=kv_r.at[i],
            device_id=sibling, device_id_type=MESH,
        ).wait_recv()

    keys = jnp.concatenate([kvr[0, :128, :], kvr[1, :128, :]], axis=1)
    values = jnp.concatenate([kvr[0, 128:, :], kvr[1, 128:, :]], axis=1)
    for h in range(4):
        query = accq[:, h * HD : (h + 1) * HD].astype(BF16)
        scores = jnp.dot(query, keys, preferred_element_type=F32) / math.sqrt(HD)
        scores = jnp.where(mask, scores, -1e30)
        top = jnp.max(scores, axis=-1, keepdims=True)
        weight = jnp.exp(scores - top)
        probs = (weight / jnp.sum(weight, axis=-1, keepdims=True)).astype(BF16)
        ctx[:, h * HD : (h + 1) * HD] = lax.dot_general(
            probs, values, (((1,), (1,)), ((), ())), preferred_element_type=F32
        ).astype(BF16)

    sent = [0] * NC

    def rs_send(j, kind, d, way, slot):
        copy = pltpu.make_async_remote_copy(
            src_ref=part.at[j, block(kind, d)], dst_ref=rsb.at[j, slot],
            send_sem=rs_s.at[j * 20 + sent[j]], recv_sem=rs_r.at[j * SLOTS + slot],
            device_id=neighbour[way], device_id_type=MESH,
        )
        sent[j] += 1
        copy.start()
        sends.append(copy)

    def rs_add(j, kind, d, slots):
        for slot in slots:
            ref = rsb.at[j, slot]
            pltpu.make_async_remote_copy(
                src_ref=ref, dst_ref=ref,
                send_sem=rs_s.at[j * 20], recv_sem=rs_r.at[j * SLOTS + slot],
                device_id=neighbour[YY], device_id_type=MESH,
            ).wait_recv()
        total = part[j, block(kind, d)].astype(F32)
        for slot in slots:
            total = total + rsb[j, slot].astype(F32)
        part[j, block(kind, d)] = total.astype(BF16)

    ships = []

    def rs_step(j, step):
        even = j % 2 == 0
        if step == 0:
            weight_ready(1 + NC + j)
            for n in range(0, KC, 512):
                part[j, :, n : n + 512] = jnp.dot(
                    ctx[...], wo[:, j * KC + n : j * KC + n + 512], preferred_element_type=F32
                ).astype(BF16)
            rs_send(j, OTHER, 4, YY, YE[4])
            if even:
                rs_send(j, OTHER, 2, ZP, QP[1])
                rs_send(j, OTHER, -2, ZM, QM[-1])
            else:
                rs_send(j, OTHER, 1, ZP, QP[0])
                rs_send(j, OTHER, -1, ZM, QM[0])
            rs_send(j, OTHER, 3, YY, YE[3])
            rs_send(j, OTHER, -3, YY, YE[-3])
            if not even:
                rs_send(j, OTHER, 2, YY, YE[2])
                rs_send(j, OTHER, -2, YY, YE[-2])
        elif step == 1:
            rs_add(j, SAME, 4, [YE[4]])
            if even:
                rs_send(j, SAME, 4, ZP, RP[3])
                rs_add(j, OTHER, 1, [QP[1]])
                rs_send(j, OTHER, 1, ZP, QP[0])
                rs_add(j, OTHER, -1, [QM[-1]])
                rs_send(j, OTHER, -1, ZM, QM[0])
            else:
                rs_send(j, SAME, 4, ZM, RM[-3])
                rs_add(j, OTHER, 0, [QP[0], QM[0]])
                rs_send(j, OTHER, 0, YY, RY)
        elif step == 2:
            if even:
                rs_add(j, SAME, -3, [YE[-3]])
                rs_send(j, SAME, -3, ZM, RM[-2])
                rs_add(j, SAME, 3, [YE[3], RP[3]])
                rs_send(j, SAME, 3, ZP, RP[2])
                rs_add(j, OTHER, 0, [QP[0], QM[0]])
                rs_send(j, OTHER, 0, YY, RY)
            else:
                rs_add(j, SAME, 3, [YE[3]])
                rs_send(j, SAME, 3, ZP, RP[2])
                rs_add(j, SAME, -3, [YE[-3], RM[-3]])
                rs_send(j, SAME, -3, ZM, RM[-2])
        elif step == 3:
            rs_add(j, SAME, 2, [RP[2]] if even else [RP[2], YE[2]])
            rs_send(j, SAME, 2, ZP, RP[1])
            rs_add(j, SAME, -2, [RM[-2]] if even else [RM[-2], YE[-2]])
            rs_send(j, SAME, -2, ZM, RM[-1])
        elif step == 4:
            rs_add(j, SAME, 1, [RP[1]])
            rs_send(j, SAME, 1, ZP, RP[0])
            rs_add(j, SAME, -1, [RM[-1]])
            rs_send(j, SAME, -1, ZM, RM[0])
        elif step == 5:
            rs_add(j, SAME, 0, [RP[0], RM[0], RY])
            ship = pltpu.make_async_remote_copy(
                src_ref=part.at[j, block(SAME, 0)], dst_ref=next_output.at[:, cols(j)],
                send_sem=sh_s.at[j], recv_sem=sh_r.at[j],
                device_id=next_sec, device_id_type=MESH,
            )
            ship.start()
            ships.append(ship)

    for r in range(max(RS_OFF) + 6):
        for j in range(NC):
            step = r - RS_OFF[j]
            if 0 <= step <= 5:
                rs_step(j, step)

    for copy in sends:
        copy.wait_send()
    for copy in far:
        copy.wait_send()
    for mine, copy in kv_copies:

        @pl.when(jnp.logical_not(mine))
        def _(copy=copy):
            copy.wait_send()

    carry.wait()
    for ship in ships:
        ship.wait()


def body(resid, pending, doc_ids, norm_gain, q_weight, kv_weight, o_weight):
    vmem = pl.BlockSpec(memory_space=pltpu.VMEM)
    hbm = pl.BlockSpec(memory_space=pl.ANY)
    dma = pltpu.SemaphoreType.DMA
    out = jax.ShapeDtypeStruct((ROWS, D), BF16)
    next_resid, next_output = pl.pallas_call(
        kernel,
        out_shape=(out, out),
        in_specs=[vmem] * 4 + [hbm] * 3,
        out_specs=(vmem, vmem),
        scratch_shapes=[
            pltpu.VMEM((NC, TOK, KC), BF16),
            pltpu.VMEM((2, D, 256), BF16),
            pltpu.VMEM((64, D), BF16),
            pltpu.VMEM((512, D), BF16),
            pltpu.VMEM((TOK, 512), F32),
            pltpu.VMEM((64, TOK), F32),
            pltpu.VMEM((64, TOK), BF16),
            pltpu.VMEM((2, 256, TOK), BF16),
            pltpu.VMEM((TOK, 512), BF16),
            pltpu.VMEM((NC, TOK, KC), BF16),
            pltpu.VMEM((NC, SLOTS, ROWS, KC), BF16),
            pltpu.VMEM((ROWS, D), BF16),
            dma((NC * 16,)),
            dma((NC * 16,)),
            dma((NC * 20,)),
            dma((NC * SLOTS,)),
            dma((8,)),
            dma((8,)),
            dma((1 + 2 * NC,)),
            dma((1 + 2 * NC,)),
            dma((1 + 2 * NC,)),
            dma((NC + 1,)),
            dma((NC + 1,)),
        ],
        compiler_params=pltpu.CompilerParams(
            collective_id=0, has_side_effects=True, vmem_limit_bytes=56 << 20
        ),
        name="module",
    )(
        resid[0], pending[0], doc_ids, norm_gain,
        q_weight[0], kv_weight[0].T, o_weight[0],
    )
    return next_resid[None], next_output[None]


def solution(mesh):
    in_specs = (
        P("section", "tp", None),
        P("section", "tp", None),
        P("section", None),
        P("section", None),
        P("section", None, "tp"),
        P("section", None, "tp"),
        P("section", "tp", None),
    )
    out_specs = (P("section", "tp", None), P("section", "tp", None))
    return jax.shard_map(body, mesh=mesh, in_specs=in_specs, out_specs=out_specs, check_vma=False)
```

time: 518 us -> 126 us (0.24)
  the two profiles are of different devices: /device:TPU:32 before, /device:TPU:6 now
where the time goes in v1:
time: 126 us
  Pallas kernels  122 us (97%)
  local copies, waits for them, and re-layouts  3.34 us (3%)
    pallas_call x1, Pallas kernels, body(): pl.pallas_call(kernel, out_shape=(out, out), in_specs=[vmem] * 4 + [hbm]...  122 us
    unnamed x2, local copies, waits for them, and re-layouts  3.34 us

profile of v1, /device:TPU:6, one launch (start us, length us, event | category | flops | bytes accessed | tf_op | source)
XLA Modules:
  0.0 125.8 jit_solution(18353217474074182496)
XLA Ops:
  0.6 121.8 %module.1 = (bf16[16,8192]{1,0:T(8,128)(2,1)}, bf16[16,8192]{1,0:T(8,128)(2,1)}) custom-call(bf16[16,8192]{1,0:T(8,128)(2,1)} %bitcast.14, bf16[16,8192]{1,0:T(8,128)(2,1)} %bitcast.15, s32[1,512]{1,0:T(1,128)} %doc_ids.1, bf16[1,8192]{1,0:T(2,128)(2,1)} %gain.1, bf16[8192,256]{1,0:T(8,128)(2,1)} %bitcast.9, bf16[32,8192]{1,0:T(8,128)(2,1)} %bitcast.11, ...), custom_call_target="tpu_custom_call" | custom-call | tf_op jit(solution)/shard_map/module/pallas_call | solution.py:384
  122.4 1.7 %copy.11 = bf16[1,16,8192]{2,1,0:T(8,128)(2,1)} copy(bf16[1,16,8192]{2,1,0:T(8,128)(2,1)} %bitcast.13) | data formatting | bytes 524288
  124.1 1.7 %copy.12 = bf16[1,16,8192]{2,1,0:T(8,128)(2,1)} copy(bf16[1,16,8192]{2,1,0:T(8,128)(2,1)} %bitcast.12) | data formatting | bytes 524288

commit v2 on v1

--- a/solution.py
+++ b/solution.py
@@ -15,21 +15,22 @@
 TOK = 256
 NC = 4
 KC = D // NC
-AG_OFF = (0, 0, 1, 2)
-RS_OFF = (0, 1, 2, 3)
+AG_LAP = 0.25
+AG_LAG = 0.5
+AG_MM = 0.5
+RS_LAP = 0.25
 MESH = pl.DeviceIdType.MESH
 F32 = jnp.float32
 BF16 = jnp.bfloat16
 SAME, OTHER = 0, 1
 ZP, ZM, YY = 0, 1, 2
 
-YE = {4: 0, 3: 1, -3: 2, 2: 3, -2: 4}
-RP = {3: 5, 2: 6, 1: 7, 0: 8}
-RM = {-3: 9, -2: 10, -1: 11, 0: 12}
-QP = {1: 13, 0: 14}
-QM = {-1: 15, 0: 16}
-RY = 17
-SLOTS = 18
+YE = {4: 0, 3: 1, 2: 2, 1: 3}
+RF = {3: 4, 2: 5, 1: 6, 0: 7}
+RB = {2: 8, 1: 9, 0: 10}
+QB = {2: 11, 1: 12, 0: 13}
+RY = 14
+SLOTS = 15
 
 
 def kernel(
@@ -120,49 +121,39 @@
             device_id=neighbour[YY], device_id_type=MESH,
         ).wait_recv()
 
-    def ag_step(j, step):
-        even = j % 2 == 0
-        if step == 0:
-            ag_send(j, SAME, 0, ZP)
-            ag_send(j, SAME, 0, ZM)
-            ag_send(j, SAME, 0, YY)
-        elif step == 1:
-            ag_wait(j, SAME, -1)
-            ag_send(j, SAME, -1, ZP)
-            ag_wait(j, SAME, 1)
-            ag_send(j, SAME, 1, ZM)
-            ag_wait(j, OTHER, 0)
-            ag_send(j, OTHER, 0, ZP)
-            ag_send(j, OTHER, 0, ZM)
-        elif step == 2:
-            ag_wait(j, SAME, -2)
-            ag_send(j, SAME, -2, ZP)
-            if not even:
-                ag_send(j, SAME, -2, YY)
-            ag_wait(j, SAME, 2)
-            ag_send(j, SAME, 2, ZM)
-            if not even:
-                ag_send(j, SAME, 2, YY)
-            ag_wait(j, OTHER, -1)
-            ag_wait(j, OTHER, 1)
-            if even:
-                ag_send(j, OTHER, -1, ZP)
-                ag_send(j, OTHER, 1, ZM)
-        elif step == 3:
-            ag_wait(j, SAME, -3)
-            if even:
-                ag_send(j, SAME, -3, ZP)
-            ag_send(j, SAME, -3, YY)
-            ag_wait(j, SAME, 3)
-            if not even:
-                ag_send(j, SAME, 3, ZM)
-            ag_send(j, SAME, 3, YY)
-        elif step == 4:
-            ag_wait(j, SAME, 4)
-            ag_send(j, SAME, 4, YY)
-        elif step == 5:
-            for d in (-2, 2, -3, 3, 4):
-                ag_wait(j, OTHER, d)
+    def ag_actions(j):
+        e = 1 if j % 2 == 0 else -1
+        fore, back = (ZP, ZM) if e == 1 else (ZM, ZP)
+
+        def begin():
+            for way in (back, fore, YY):
+                ag_send(j, SAME, 0, way)
+
+        def relay(kind, d, *ways):
+            def act():
+                ag_wait(j, kind, d)
+                for way in ways:
+                    ag_send(j, kind, d, way)
+
+            return act
+
+        def finish():
+            for kind, d in ((SAME, -3), (OTHER, 1), (OTHER, 2), (OTHER, 3), (OTHER, -3), (OTHER, 4)):
+                ag_wait(j, kind, d * e if d != 4 else 4)
+
+        return [
+            (0, begin),
+            (1, relay(SAME, e, back, YY)),
+            (1, relay(SAME, -e, fore)),
+            (1 + AG_LAG, relay(OTHER, 0, fore)),
+            (2, relay(SAME, 2 * e, back, YY)),
+            (2, relay(SAME, -2 * e, fore)),
+            (2 + AG_LAG, relay(OTHER, -e, fore)),
+            (3, relay(SAME, 3 * e, back, YY)),
+            (3 + AG_LAG, relay(OTHER, -2 * e, fore)),
+            (4, relay(SAME, 4, YY)),
+            (5, finish),
+        ]
 
     def weight_ready(i):
         local[i].wait()
@@ -186,18 +177,24 @@
             span = slice(cc * 256, (cc + 1) * 256)
             accq[:, span] = term if j == 0 else accq[:, span] + term
 
-    for r in range(max(AG_OFF) + 6):
-        for j in range(NC):
-            step = r - AG_OFF[j]
-            if 0 <= step <= 5:
-                ag_step(j, step)
-        if r == 0:
-            for copy in far:
-                copy.start()
-        for j in range(NC - 1):
-            if r - AG_OFF[j] == 5:
-                project_kv(j)
-                project_q(j)
+    def send_weights():
+        for copy in far:
+            copy.start()
+
+    def project(j):
+        def act():
+            project_kv(j)
+            project_q(j)
+
+        return act
+
+    actions = [(0, send_weights)]
+    for j in range(NC):
+        actions += [(j * AG_LAP + when, act) for when, act in ag_actions(j)]
+        if j < NC - 1:
+            actions.append((j * AG_LAP + 5 + AG_MM, project(j)))
+    for _, act in sorted(actions, key=lambda item: item[0]):
+        act()
 
     project_kv(NC - 1)
     kvs[...] = acckv[...].astype(BF16)
@@ -290,63 +287,32 @@
 
     ships = []
 
-    def rs_step(j, step):
-        even = j % 2 == 0
-        if step == 0:
+    def rs_actions(j):
+        e = 1 if j % 2 == 0 else -1
+        fore, back = (ZP, ZM) if e == 1 else (ZM, ZP)
+
+        def begin():
             weight_ready(1 + NC + j)
             for n in range(0, KC, 512):
                 part[j, :, n : n + 512] = jnp.dot(
                     ctx[...], wo[:, j * KC + n : j * KC + n + 512], preferred_element_type=F32
                 ).astype(BF16)
             rs_send(j, OTHER, 4, YY, YE[4])
-            if even:
-                rs_send(j, OTHER, 2, ZP, QP[1])
-                rs_send(j, OTHER, -2, ZM, QM[-1])
-            else:
-                rs_send(j, OTHER, 1, ZP, QP[0])
-                rs_send(j, OTHER, -1, ZM, QM[0])
-            rs_send(j, OTHER, 3, YY, YE[3])
-            rs_send(j, OTHER, -3, YY, YE[-3])
-            if not even:
-                rs_send(j, OTHER, 2, YY, YE[2])
-                rs_send(j, OTHER, -2, YY, YE[-2])
-        elif step == 1:
-            rs_add(j, SAME, 4, [YE[4]])
-            if even:
-                rs_send(j, SAME, 4, ZP, RP[3])
-                rs_add(j, OTHER, 1, [QP[1]])
-                rs_send(j, OTHER, 1, ZP, QP[0])
-                rs_add(j, OTHER, -1, [QM[-1]])
-                rs_send(j, OTHER, -1, ZM, QM[0])
-            else:
-                rs_send(j, SAME, 4, ZM, RM[-3])
-                rs_add(j, OTHER, 0, [QP[0], QM[0]])
-                rs_send(j, OTHER, 0, YY, RY)
-        elif step == 2:
-            if even:
-                rs_add(j, SAME, -3, [YE[-3]])
-                rs_send(j, SAME, -3, ZM, RM[-2])
-                rs_add(j, SAME, 3, [YE[3], RP[3]])
-                rs_send(j, SAME, 3, ZP, RP[2])
-                rs_add(j, OTHER, 0, [QP[0], QM[0]])
-                rs_send(j, OTHER, 0, YY, RY)
-            else:
-                rs_add(j, SAME, 3, [YE[3]])
-                rs_send(j, SAME, 3, ZP, RP[2])
-                rs_add(j, SAME, -3, [YE[-3], RM[-3]])
-                rs_send(j, SAME, -3, ZM, RM[-2])
-        elif step == 3:
-            rs_add(j, SAME, 2, [RP[2]] if even else [RP[2], YE[2]])
-            rs_send(j, SAME, 2, ZP, RP[1])
-            rs_add(j, SAME, -2, [RM[-2]] if even else [RM[-2], YE[-2]])
-            rs_send(j, SAME, -2, ZM, RM[-1])
-        elif step == 4:
-            rs_add(j, SAME, 1, [RP[1]])
-            rs_send(j, SAME, 1, ZP, RP[0])
-            rs_add(j, SAME, -1, [RM[-1]])
-            rs_send(j, SAME, -1, ZM, RM[0])
-        elif step == 5:
-            rs_add(j, SAME, 0, [RP[0], RM[0], RY])
+            rs_send(j, OTHER, -3 * e, back, QB[2])
+            rs_send(j, OTHER, 3 * e, YY, YE[3])
+            rs_send(j, SAME, -3 * e, back, RB[2])
+            rs_send(j, OTHER, 2 * e, YY, YE[2])
+            rs_send(j, OTHER, e, YY, YE[1])
+
+        def relay(kind, d, slots, way, slot):
+            def act():
+                rs_add(j, kind, d, slots)
+                rs_send(j, kind, d, way, slot)
+
+            return act
+
+        def finish():
+            rs_add(j, SAME, 0, [RF[0], RB[0], RY])
             ship = pltpu.make_async_remote_copy(
                 src_ref=part.at[j, block(SAME, 0)], dst_ref=next_output.at[:, cols(j)],
                 send_sem=sh_s.at[j], recv_sem=sh_r.at[j],
@@ -355,11 +321,25 @@
             ship.start()
             ships.append(ship)
 
-    for r in range(max(RS_OFF) + 6):
-        for j in range(NC):
-            step = r - RS_OFF[j]
-            if 0 <= step <= 5:
-                rs_step(j, step)
+        return [
+            (0, begin),
+            (1, relay(SAME, 4, [YE[4]], fore, RF[3])),
+            (1, relay(OTHER, -2 * e, [QB[2]], back, QB[1])),
+            (1, relay(SAME, -2 * e, [RB[2]], back, RB[1])),
+            (2, relay(SAME, 3 * e, [YE[3], RF[3]], fore, RF[2])),
+            (2, relay(OTHER, -e, [QB[1]], back, QB[0])),
+            (2, relay(SAME, -e, [RB[1]], back, RB[0])),
+            (3, relay(SAME, 2 * e, [YE[2], RF[2]], fore, RF[1])),
+            (3, relay(OTHER, 0, [QB[0]], YY, RY)),
+            (4, relay(SAME, e, [YE[1], RF[1]], fore, RF[0])),
+            (5, finish),
+        ]
+
+    actions = []
+    for j in range(NC):
+        actions += [(j * RS_LAP + when, act) for when, act in rs_actions(j)]
+    for _, act in sorted(actions, key=lambda item: item[0]):
+        act()
 
     for copy in sends:
         copy.wait_send()

time: 126 us -> 115 us (0.913)
  the two profiles are of different devices: /device:TPU:6 before, /device:TPU:32 now
where the time goes in v2:
time: 115 us
  Pallas kernels  111 us (97%)
  local copies, waits for them, and re-layouts  3.34 us (3%)
    pallas_call x1, Pallas kernels, body(): pl.pallas_call(kernel, out_shape=(out, out), in_specs=[vmem] * 4 + [hbm]...  111 us
    unnamed x2, local copies, waits for them, and re-layouts  3.34 us

profile of v2, /device:TPU:32, one launch (start us, length us, event | category | flops | bytes accessed | tf_op | source)
XLA Modules:
  0.0 115.1 jit_solution(9990971280916656321)
XLA Ops:
  0.6 111.2 %module.1 = (bf16[16,8192]{1,0:T(8,128)(2,1)}, bf16[16,8192]{1,0:T(8,128)(2,1)}) custom-call(bf16[16,8192]{1,0:T(8,128)(2,1)} %bitcast.14, bf16[16,8192]{1,0:T(8,128)(2,1)} %bitcast.15, s32[1,512]{1,0:T(1,128)} %doc_ids.1, bf16[1,8192]{1,0:T(2,128)(2,1)} %gain.1, bf16[8192,256]{1,0:T(8,128)(2,1)} %bitcast.9, bf16[32,8192]{1,0:T(8,128)(2,1)} %bitcast.11, ...), custom_call_target="tpu_custom_call" | custom-call | tf_op jit(solution)/shard_map/module/pallas_call | solution.py:364
  111.8 1.7 %copy.11 = bf16[1,16,8192]{2,1,0:T(8,128)(2,1)} copy(bf16[1,16,8192]{2,1,0:T(8,128)(2,1)} %bitcast.13) | data formatting | bytes 524288
  113.5 1.7 %copy.12 = bf16[1,16,8192]{2,1,0:T(8,128)(2,1)} copy(bf16[1,16,8192]{2,1,0:T(8,128)(2,1)} %bitcast.12) | data formatting | bytes 524288

commit v3 on v2

--- a/solution.py
+++ b/solution.py
@@ -15,10 +15,14 @@
 TOK = 256
 NC = 4
 KC = D // NC
+VMEM = 56
+FINISH = 1
 AG_LAP = 0.25
-AG_LAG = 0.5
+AG_LAG = 1.5
 AG_MM = 0.5
-RS_LAP = 0.25
+RS_LAP = 0
+RS_Y = (0.1, 0.2, 0.3)
+CARRY = 5.12
 MESH = pl.DeviceIdType.MESH
 F32 = jnp.float32
 BF16 = jnp.bfloat16
@@ -29,15 +33,14 @@
 RF = {3: 4, 2: 5, 1: 6, 0: 7}
 RB = {2: 8, 1: 9, 0: 10}
 QB = {2: 11, 1: 12, 0: 13}
-RY = 14
-SLOTS = 15
+SLOTS = 14
 
 
 def kernel(
     resid, pending, doc_ids, gain, wq_hbm, wkv_hbm, wo_hbm,
-    next_resid, next_output,
+    next_resid, fin,
     xg, wq, wkv, wo, accq, acckv, kvs, kvr, ctx, part, rsb, carr,
-    ag_s, ag_r, rs_s, rs_r, kv_s, kv_r, lw, ws, wr, sh_s, sh_r,
+    ag_s, ag_r, rs_s, rs_r, kv_s, kv_r, lw, ws, wr, sh_s, sh_r, fin_s, fin_r,
 ):
     sec = lax.axis_index("section")
     t = lax.axis_index("tp")
@@ -52,8 +55,9 @@
         at(z, 1 - yh, c),
     )
     sibling = at(z, yh, 1 - c)
-    next_sec = ((sec + 1) % 8, t)
-    prev_sec = ((sec + 7) % 8, t)
+    across = (z * 2 + 1 - yh) * 2 + c
+    after, before = (sec + 1) % 8, (sec + 7) % 8
+    heirs = ((after, t), (after, across))
 
     def block(kind, d):
         b = ((z + d + Z) % Z) * 2 + (yh if kind == SAME else 1 - yh)
@@ -62,7 +66,7 @@
     barrier = pltpu.get_barrier_semaphore()
     for o in range(1, 32):
         pl.semaphore_signal(barrier, inc=1, device_id=(sec, (t + o) % 32), device_id_type=MESH)
-    for dev in (next_sec, prev_sec):
+    for dev in (*heirs, (before, t), (before, across)):
         pl.semaphore_signal(barrier, inc=1, device_id=dev, device_id_type=MESH)
 
     def cols(j):
@@ -94,7 +98,7 @@
             piece * scale * gain[:, j * KC : (j + 1) * KC].astype(F32)
         ).astype(BF16)
 
-    pl.semaphore_wait(barrier, 33)
+    pl.semaphore_wait(barrier, 35)
 
     sends = []
 
@@ -177,18 +181,26 @@
             span = slice(cc * 256, (cc + 1) * 256)
             accq[:, span] = term if j == 0 else accq[:, span] + term
 
+    carry = pltpu.make_async_remote_copy(
+        src_ref=carr, dst_ref=next_resid,
+        send_sem=sh_s, recv_sem=sh_r,
+        device_id=heirs[0], device_id_type=MESH,
+    )
+
+    def send_carry():
+        carr[...] = (resid[...].astype(F32) + pending[...].astype(F32)).astype(BF16)
+        carry.start()
+
     def send_weights():
         for copy in far:
             copy.start()
 
     def project(j):
-        def act():
-            project_kv(j)
-            project_q(j)
-
-        return act
+        return lambda: project_kv(j)
 
     actions = [(0, send_weights)]
+    if CARRY < 5:
+        actions.append((CARRY, send_carry))
     for j in range(NC):
         actions += [(j * AG_LAP + when, act) for when, act in ag_actions(j)]
         if j < NC - 1:
@@ -199,35 +211,29 @@
     project_kv(NC - 1)
     kvs[...] = acckv[...].astype(BF16)
     kv_rows = pl.ds(pl.multiple_of((z // 4) * 128 + yh * 64, 64), 64)
-    kv_index = (z // 4) * 4 + yh * 2 + c
     kv_copies = []
-    for n in range(8):
-        zz, yy, cc = 2 * (z % 4) + n // 4, (n // 2) % 2, n % 2
-        mine = (zz == z) & (yy == yh) & (cc == c)
+    for yy in range(2):
+        zz = 2 * (z % 4) + z // 4
+        mine = (zz == z) & (yy == yh)
         copy = pltpu.make_async_remote_copy(
             src_ref=kvs, dst_ref=kvr.at[c, kv_rows],
-            send_sem=kv_s.at[n], recv_sem=kv_r.at[kv_index],
-            device_id=at(zz, yy, cc), device_id_type=MESH,
+            send_sem=kv_s.at[yy], recv_sem=kv_r.at[yh],
+            device_id=at(zz, yy, c), device_id_type=MESH,
         )
         kv_copies.append((mine, copy))
 
         @pl.when(mine)
         def _():
-            pltpu.make_async_copy(kvs, kvr.at[c, kv_rows], kv_r.at[kv_index]).start()
+            pltpu.make_async_copy(kvs, kvr.at[c, kv_rows], kv_r.at[yh]).start()
 
         @pl.when(jnp.logical_not(mine))
         def _(copy=copy):
             copy.start()
 
-    carr[...] = (resid[...].astype(F32) + pending[...].astype(F32)).astype(BF16)
-    carry = pltpu.make_async_remote_copy(
-        src_ref=carr, dst_ref=next_resid,
-        send_sem=sh_s.at[NC], recv_sem=sh_r.at[NC],
-        device_id=next_sec, device_id_type=MESH,
-    )
-    carry.start()
-
-    project_q(NC - 1)
+    if CARRY == 5.1:
+        send_carry()
+    for j in range(NC - 1):
+        project_q(j)
 
     docs = doc_ids[...].astype(F32)
     row = lax.broadcasted_iota(jnp.int32, (TOK, 1), 0)
@@ -240,13 +246,44 @@
         first = jnp.maximum(first, jnp.where(mine_at >= begin, begin, 0.0))
     mask = (key_at <= mine_at) & (key_at >= first)
 
-    for i in range(8):
-        ref = kvr.at[i % 2, pl.ds((i // 2) * 64, 64)]
+    twin = at(z + 1 - 2 * (z % 2), yh, c)
+
+    def kv_relay(i, kind, half, targets):
+        rows = pl.ds(pl.multiple_of(kind * 128 + half * 64, 64), 64)
+        ref = kvr.at[c, rows]
         pltpu.make_async_remote_copy(
             src_ref=ref, dst_ref=ref, send_sem=kv_s.at[0], recv_sem=kv_r.at[i],
             device_id=sibling, device_id_type=MESH,
         ).wait_recv()
-
+        for n, (dev, slot) in enumerate(targets):
+            copy = pltpu.make_async_remote_copy(
+                src_ref=ref, dst_ref=ref,
+                send_sem=kv_s.at[2 + 2 * i + n], recv_sem=kv_r.at[slot],
+                device_id=dev, device_id_type=MESH,
+            )
+            copy.start()
+            sends.append(copy)
+
+    for half in range(2):
+        kv_relay(half, z % 2, half, [(twin, 2 + half), (sibling, 4 + half)])
+    if CARRY == 5.12:
+        send_carry()
+    project_q(NC - 1)
+    for half in range(2):
+        kv_relay(2 + half, 1 - z % 2, half, [(sibling, 6 + half)])
+    if CARRY == 5.15:
+        send_carry()
+    for i in range(4):
+        kind = z % 2 if i < 2 else 1 - z % 2
+        rows = pl.ds(pl.multiple_of(kind * 128 + (i % 2) * 64, 64), 64)
+        ref = kvr.at[1 - c, rows]
+        pltpu.make_async_remote_copy(
+            src_ref=ref, dst_ref=ref, send_sem=kv_s.at[0], recv_sem=kv_r.at[4 + i],
+            device_id=sibling, device_id_type=MESH,
+        ).wait_recv()
+
+    if CARRY == 5.2:
+        send_carry()
     keys = jnp.concatenate([kvr[0, :128, :], kvr[1, :128, :]], axis=1)
     values = jnp.concatenate([kvr[0, 128:, :], kvr[1, 128:, :]], axis=1)
     for h in range(4):
@@ -285,7 +322,16 @@
             total = total + rsb[j, slot].astype(F32)
         part[j, block(kind, d)] = total.astype(BF16)
 
-    ships = []
+    def hand_on(j, which):
+        copy = pltpu.make_async_remote_copy(
+            src_ref=part.at[j, block(which, 0)], dst_ref=fin.at[which, :, cols(j)],
+            send_sem=fin_s.at[2 * j + which], recv_sem=fin_r.at[2 * j + which],
+            device_id=heirs[which], device_id_type=MESH,
+        )
+        copy.start()
+        handed.append(copy)
+
+    handed = []
 
     def rs_actions(j):
         e = 1 if j % 2 == 0 else -1
@@ -299,10 +345,10 @@
                 ).astype(BF16)
             rs_send(j, OTHER, 4, YY, YE[4])
             rs_send(j, OTHER, -3 * e, back, QB[2])
-            rs_send(j, OTHER, 3 * e, YY, YE[3])
             rs_send(j, SAME, -3 * e, back, RB[2])
-            rs_send(j, OTHER, 2 * e, YY, YE[2])
-            rs_send(j, OTHER, e, YY, YE[1])
+
+        def cross(d):
+            return lambda: rs_send(j, OTHER, d * e, YY, YE[d])
 
         def relay(kind, d, slots, way, slot):
             def act():
@@ -311,18 +357,18 @@
 
             return act
 
-        def finish():
-            rs_add(j, SAME, 0, [RF[0], RB[0], RY])
-            ship = pltpu.make_async_remote_copy(
-                src_ref=part.at[j, block(SAME, 0)], dst_ref=next_output.at[:, cols(j)],
-                send_sem=sh_s.at[j], recv_sem=sh_r.at[j],
-                device_id=next_sec, device_id_type=MESH,
-            )
-            ship.start()
-            ships.append(ship)
+        def finish(kind, slots):
+            def act():
+                rs_add(j, kind, 0, slots)
+                hand_on(j, kind)
+
+            return act
 
         return [
             (0, begin),
+            (RS_Y[0], cross(3)),
+            (RS_Y[1], cross(2)),
+            (RS_Y[2], cross(1)),
             (1, relay(SAME, 4, [YE[4]], fore, RF[3])),
             (1, relay(OTHER, -2 * e, [QB[2]], back, QB[1])),
             (1, relay(SAME, -2 * e, [RB[2]], back, RB[1])),
@@ -330,16 +376,27 @@
             (2, relay(OTHER, -e, [QB[1]], back, QB[0])),
             (2, relay(SAME, -e, [RB[1]], back, RB[0])),
             (3, relay(SAME, 2 * e, [YE[2], RF[2]], fore, RF[1])),
-            (3, relay(OTHER, 0, [QB[0]], YY, RY)),
+            (3, finish(OTHER, [QB[0]])),
             (4, relay(SAME, e, [YE[1], RF[1]], fore, RF[0])),
-            (5, finish),
+            (5, finish(SAME, [RF[0], RB[0]])),
         ]
 
     actions = []
+    if CARRY >= 6:
+        actions.append((CARRY - 6, send_carry))
     for j in range(NC):
         actions += [(j * RS_LAP + when, act) for when, act in rs_actions(j)]
     for _, act in sorted(actions, key=lambda item: item[0]):
         act()
+
+    for j in range(NC):
+        for which in range(2):
+            ref = fin.at[which, :, cols(j)]
+            pltpu.make_async_remote_copy(
+                src_ref=ref, dst_ref=ref,
+                send_sem=fin_s.at[0], recv_sem=fin_r.at[2 * j + which],
+                device_id=heirs[0], device_id_type=MESH,
+            ).wait_recv()
 
     for copy in sends:
         copy.wait_send()
@@ -352,20 +409,27 @@
             copy.wait_send()
 
     carry.wait()
-    for ship in ships:
-        ship.wait()
+    for copy in handed:
+        copy.wait_send()
+
+
+def finish_kernel(carried, sums, next_resid, next_output):
+    next_resid[...] = carried[...]
+    next_output[...] = (sums[0].astype(F32) + sums[1].astype(F32)).astype(BF16)
 
 
 def body(resid, pending, doc_ids, norm_gain, q_weight, kv_weight, o_weight):
     vmem = pl.BlockSpec(memory_space=pltpu.VMEM)
-    hbm = pl.BlockSpec(memory_space=pl.ANY)
+    hbm = pl.BlockSpec(memory_space=pltpu.HBM)
     dma = pltpu.SemaphoreType.DMA
-    out = jax.ShapeDtypeStruct((ROWS, D), BF16)
-    next_resid, next_output = pl.pallas_call(
+    carried, sums = pl.pallas_call(
         kernel,
-        out_shape=(out, out),
+        out_shape=(
+            jax.ShapeDtypeStruct((ROWS, D), BF16),
+            jax.ShapeDtypeStruct((2, ROWS, D), BF16),
+        ),
         in_specs=[vmem] * 4 + [hbm] * 3,
-        out_specs=(vmem, vmem),
+        out_specs=(hbm, hbm),
         scratch_shapes=[
             pltpu.VMEM((NC, TOK, KC), BF16),
             pltpu.VMEM((2, D, 256), BF16),
@@ -383,22 +447,35 @@
             dma((NC * 16,)),
             dma((NC * 20,)),
             dma((NC * SLOTS,)),
-            dma((8,)),
+            dma((10,)),
             dma((8,)),
             dma((1 + 2 * NC,)),
             dma((1 + 2 * NC,)),
             dma((1 + 2 * NC,)),
-            dma((NC + 1,)),
-            dma((NC + 1,)),
+            dma,
+            dma,
+            dma((2 * NC,)),
+            dma((2 * NC,)),
         ],
         compiler_params=pltpu.CompilerParams(
-            collective_id=0, has_side_effects=True, vmem_limit_bytes=56 << 20
+            collective_id=0, has_side_effects=True, vmem_limit_bytes=VMEM << 20
         ),
         name="module",
     )(
         resid[0], pending[0], doc_ids, norm_gain,
         q_weight[0], kv_weight[0].T, o_weight[0],
     )
+    if FINISH == 0:
+        return carried[None], (sums[0].astype(F32) + sums[1].astype(F32)).astype(BF16)[None]
+    out = jax.ShapeDtypeStruct((ROWS, D), BF16)
+    next_resid, next_output = pl.pallas_call(
+        finish_kernel,
+        out_shape=(out, out),
+        in_specs=[vmem, vmem],
+        out_specs=(vmem, vmem),
+        compiler_params=pltpu.CompilerParams(vmem_limit_bytes=VMEM << 20),
+        name="finish",
+    )(carried, sums)
     return next_resid[None], next_output[None]
 
 

time: 115 us -> 105 us (0.913); the launches traced: 115 us -> 103 us
  Pallas kernels: 111 us -> 102 us
  local copies, waits for them, and re-layouts: 3.34 us -> 0 us
    pallas_call x1 -> x2, Pallas kernels: 111 us -> 102 us  [the longest x1 101 us: body(): pl.pallas_call(kernel, out_shape=(jax.ShapeDtypeStruct((ROWS, D), BF16),...]
    unnamed x2 -> x0, local copies, waits for them, and re-layouts: 3.34 us -> none
where the time goes in v3:
time: 105 us; the launch traced here: 103 us
  Pallas kernels  102 us (97%)
    pallas_call x1, Pallas kernels, body(): pl.pallas_call(kernel, out_shape=(jax.ShapeDtypeStruct((ROWS, D), BF16),...  101 us

profile of v3, /device:TPU:32, one launch (start us, length us, event | category | flops | bytes accessed | tf_op | source)
XLA Modules:
  0.0 103.1 jit_solution(7307685218500462760)
XLA Ops:
  0.6 100.6 %module.1 = (bf16[16,8192]{1,0:T(8,128)(2,1)}, bf16[2,16,8192]{2,1,0:T(8,128)(2,1)}) custom-call(bf16[16,8192]{1,0:T(8,128)(2,1)} %bitcast.12, bf16[16,8192]{1,0:T(8,128)(2,1)} %bitcast.13, s32[1,512]{1,0:T(1,128)} %doc_ids.1, bf16[1,8192]{1,0:T(2,128)(2,1)} %gain.1, bf16[8192,256]{1,0:T(8,128)(2,1)} %bitcast.9, bf16[32,8192]{1,0:T(8,128)(2,1)} %bitcast.11, ...), custom_call_target="tpu_custom_call" | custom-call | tf_op jit(solution)/shard_map/module/pallas_call | solution.py:425
  101.2 1.9 %finish.1 = (bf16[16,8192]{1,0:T(8,128)(2,1)}, bf16[16,8192]{1,0:T(8,128)(2,1)}) custom-call(bf16[16,8192]{1,0:T(8,128)(2,1)} %get-tuple-element.6.carried, bf16[2,16,8192]{2,1,0:T(8,128)(2,1)} %get-tuple-element.7.sums), custom_call_target="tpu_custom_call" | custom-call | tf_op jit(solution)/shard_map/finish/pallas_call | solution.py:471

commit v4 on v3

--- a/solution.py
+++ b/solution.py
@@ -1,6 +1,4 @@
 import functools
-import math
-
 import jax
 import jax.numpy as jnp
 from jax import lax
@@ -18,9 +16,14 @@
 VMEM = 56
 FINISH = 1
 AG_LAP = 0.25
-AG_LAG = 1.5
+AG_LAG = 1.1
+KV_ORDER = (0, 1, 2, 3)
+T_F = (1, 2, 3, 4)
+T_Q = (1, 2)
+T_B = (0, 1.5, 2.5)
 AG_MM = 0.5
 RS_LAP = 0
+RS_Q = 3
 RS_Y = (0.1, 0.2, 0.3)
 CARRY = 5.12
 MESH = pl.DeviceIdType.MESH
@@ -92,12 +95,6 @@
 
     stream = resid[...].astype(F32)
     scale = lax.rsqrt(jnp.mean(stream * stream, axis=-1, keepdims=True) + 1e-05)
-    for j in range(NC):
-        piece = resid[:, j * KC : (j + 1) * KC].astype(F32)
-        xg[j, block(SAME, 0)] = (
-            piece * scale * gain[:, j * KC : (j + 1) * KC].astype(F32)
-        ).astype(BF16)
-
     pl.semaphore_wait(barrier, 35)
 
     sends = []
@@ -130,6 +127,10 @@
         fore, back = (ZP, ZM) if e == 1 else (ZM, ZP)
 
         def begin():
+            piece = resid[:, j * KC : (j + 1) * KC].astype(F32)
+            xg[j, block(SAME, 0)] = (
+                piece * scale * gain[:, j * KC : (j + 1) * KC].astype(F32)
+            ).astype(BF16)
             for way in (back, fore, YY):
                 ag_send(j, SAME, 0, way)
 
@@ -212,19 +213,19 @@
     kvs[...] = acckv[...].astype(BF16)
     kv_rows = pl.ds(pl.multiple_of((z // 4) * 128 + yh * 64, 64), 64)
     kv_copies = []
-    for yy in range(2):
-        zz = 2 * (z % 4) + z // 4
+    for n in range(4):
+        zz, yy = 2 * (z % 4) + n // 2, n % 2
         mine = (zz == z) & (yy == yh)
         copy = pltpu.make_async_remote_copy(
             src_ref=kvs, dst_ref=kvr.at[c, kv_rows],
-            send_sem=kv_s.at[yy], recv_sem=kv_r.at[yh],
+            send_sem=kv_s.at[n], recv_sem=kv_r.at[z // 4 * 2 + yh],
             device_id=at(zz, yy, c), device_id_type=MESH,
         )
         kv_copies.append((mine, copy))
 
         @pl.when(mine)
         def _():
-            pltpu.make_async_copy(kvs, kvr.at[c, kv_rows], kv_r.at[yh]).start()
+            pltpu.make_async_copy(kvs, kvr.at[c, kv_rows], kv_r.at[z // 4 * 2 + yh]).start()
 
         @pl.when(jnp.logical_not(mine))
         def _(copy=copy):
@@ -246,36 +247,32 @@
         first = jnp.maximum(first, jnp.where(mine_at >= begin, begin, 0.0))
     mask = (key_at <= mine_at) & (key_at >= first)
 
-    twin = at(z + 1 - 2 * (z % 2), yh, c)
 
     def kv_relay(i, kind, half, targets):
-        rows = pl.ds(pl.multiple_of(kind * 128 + half * 64, 64), 64)
+        rows = pl.ds(kind * 128 + half * 64, 64)
         ref = kvr.at[c, rows]
         pltpu.make_async_remote_copy(
             src_ref=ref, dst_ref=ref, send_sem=kv_s.at[0], recv_sem=kv_r.at[i],
             device_id=sibling, device_id_type=MESH,
         ).wait_recv()
-        for n, (dev, slot) in enumerate(targets):
+        for dev, slot in targets:
             copy = pltpu.make_async_remote_copy(
                 src_ref=ref, dst_ref=ref,
-                send_sem=kv_s.at[2 + 2 * i + n], recv_sem=kv_r.at[slot],
+                send_sem=kv_s.at[4 + i], recv_sem=kv_r.at[slot],
                 device_id=dev, device_id_type=MESH,
             )
             copy.start()
             sends.append(copy)
 
-    for half in range(2):
-        kv_relay(half, z % 2, half, [(twin, 2 + half), (sibling, 4 + half)])
     if CARRY == 5.12:
         send_carry()
     project_q(NC - 1)
-    for half in range(2):
-        kv_relay(2 + half, 1 - z % 2, half, [(sibling, 6 + half)])
+    for i in KV_ORDER:
+        kv_relay(i, i // 2, i % 2, [(sibling, 4 + i)])
     if CARRY == 5.15:
         send_carry()
     for i in range(4):
-        kind = z % 2 if i < 2 else 1 - z % 2
-        rows = pl.ds(pl.multiple_of(kind * 128 + (i % 2) * 64, 64), 64)
+        rows = pl.ds(i * 64, 64)
         ref = kvr.at[1 - c, rows]
         pltpu.make_async_remote_copy(
             src_ref=ref, dst_ref=ref, send_sem=kv_s.at[0], recv_sem=kv_r.at[4 + i],
@@ -288,11 +285,11 @@
     values = jnp.concatenate([kvr[0, 128:, :], kvr[1, 128:, :]], axis=1)
     for h in range(4):
         query = accq[:, h * HD : (h + 1) * HD].astype(BF16)
-        scores = jnp.dot(query, keys, preferred_element_type=F32) / math.sqrt(HD)
+        scores = jnp.dot(query, keys, preferred_element_type=F32) * HD**-0.5
         scores = jnp.where(mask, scores, -1e30)
         top = jnp.max(scores, axis=-1, keepdims=True)
         weight = jnp.exp(scores - top)
-        probs = (weight / jnp.sum(weight, axis=-1, keepdims=True)).astype(BF16)
+        probs = (weight * (1.0 / jnp.sum(weight, axis=-1, keepdims=True))).astype(BF16)
         ctx[:, h * HD : (h + 1) * HD] = lax.dot_general(
             probs, values, (((1,), (1,)), ((), ())), preferred_element_type=F32
         ).astype(BF16)
@@ -345,7 +342,6 @@
                 ).astype(BF16)
             rs_send(j, OTHER, 4, YY, YE[4])
             rs_send(j, OTHER, -3 * e, back, QB[2])
-            rs_send(j, SAME, -3 * e, back, RB[2])
 
         def cross(d):
             return lambda: rs_send(j, OTHER, d * e, YY, YE[d])
@@ -369,15 +365,16 @@
             (RS_Y[0], cross(3)),
             (RS_Y[1], cross(2)),
             (RS_Y[2], cross(1)),
-            (1, relay(SAME, 4, [YE[4]], fore, RF[3])),
-            (1, relay(OTHER, -2 * e, [QB[2]], back, QB[1])),
-            (1, relay(SAME, -2 * e, [RB[2]], back, RB[1])),
-            (2, relay(SAME, 3 * e, [YE[3], RF[3]], fore, RF[2])),
-            (2, relay(OTHER, -e, [QB[1]], back, QB[0])),
-            (2, relay(SAME, -e, [RB[1]], back, RB[0])),
-            (3, relay(SAME, 2 * e, [YE[2], RF[2]], fore, RF[1])),
-            (3, finish(OTHER, [QB[0]])),
-            (4, relay(SAME, e, [YE[1], RF[1]], fore, RF[0])),
+            (T_B[0], lambda: rs_send(j, SAME, -3 * e, back, RB[2])),
+            (T_F[0], relay(SAME, 4, [YE[4]], fore, RF[3])),
+            (T_Q[0], relay(OTHER, -2 * e, [QB[2]], back, QB[1])),
+            (T_B[1], relay(SAME, -2 * e, [RB[2]], back, RB[1])),
+            (T_F[1], relay(SAME, 3 * e, [YE[3], RF[3]], fore, RF[2])),
+            (T_Q[1], relay(OTHER, -e, [QB[1]], back, QB[0])),
+            (T_B[2], relay(SAME, -e, [RB[1]], back, RB[0])),
+            (T_F[2], relay(SAME, 2 * e, [YE[2], RF[2]], fore, RF[1])),
+            (RS_Q, finish(OTHER, [QB[0]])),
+            (T_F[3], relay(SAME, e, [YE[1], RF[1]], fore, RF[0])),
             (5, finish(SAME, [RF[0], RB[0]])),
         ]
 

time: 105 us -> 102 us (0.971)
  Pallas kernels: 102 us -> 99.7 us
    pallas_call x1, Pallas kernels: 101 us -> 97.7 us  [body(): pl.pallas_call(kernel, out_shape=(jax.ShapeDtypeStruct((ROWS, D), BF16),...]
where the time goes in v4:
time: 102 us; the launch traced here: 100 us
  Pallas kernels  99.7 us (98%)
    pallas_call x1, Pallas kernels, body(): pl.pallas_call(kernel, out_shape=(jax.ShapeDtypeStruct((ROWS, D), BF16),...  97.7 us

profile of v4, /device:TPU:32, one launch (start us, length us, event | category | flops | bytes accessed | tf_op | source)
XLA Modules:
  0.0 100.3 jit_solution(8359092397856205860)
XLA Ops:
  0.6 97.7 %module.1 = (bf16[16,8192]{1,0:T(8,128)(2,1)}, bf16[2,16,8192]{2,1,0:T(8,128)(2,1)}) custom-call(bf16[16,8192]{1,0:T(8,128)(2,1)} %bitcast.12, bf16[16,8192]{1,0:T(8,128)(2,1)} %bitcast.13, s32[1,512]{1,0:T(1,128)} %doc_ids.1, bf16[1,8192]{1,0:T(2,128)(2,1)} %gain.1, bf16[8192,256]{1,0:T(8,128)(2,1)} %bitcast.9, bf16[32,8192]{1,0:T(8,128)(2,1)} %bitcast.11, ...), custom_call_target="tpu_custom_call" | custom-call | tf_op jit(solution)/shard_map/module/pallas_call | solution.py:422
  98.4 1.9 %finish.1 = (bf16[16,8192]{1,0:T(8,128)(2,1)}, bf16[16,8192]{1,0:T(8,128)(2,1)}) custom-call(bf16[16,8192]{1,0:T(8,128)(2,1)} %get-tuple-element.6.carried, bf16[2,16,8192]{2,1,0:T(8,128)(2,1)} %get-tuple-element.7.sums), custom_call_target="tpu_custom_call" | custom-call | tf_op jit(solution)/shard_map/finish/pallas_call | solution.py:468

commit v5 on v4

--- a/solution.py
+++ b/solution.py
@@ -14,7 +14,6 @@
 NC = 4
 KC = D // NC
 VMEM = 56
-FINISH = 1
 AG_LAP = 0.25
 AG_LAG = 1.1
 KV_ORDER = (0, 1, 2, 3)
@@ -23,9 +22,8 @@
 T_B = (0, 1.5, 2.5)
 AG_MM = 0.5
 RS_LAP = 0
-RS_Q = 3
+RS_Q = 2.5
 RS_Y = (0.1, 0.2, 0.3)
-CARRY = 5.12
 MESH = pl.DeviceIdType.MESH
 F32 = jnp.float32
 BF16 = jnp.bfloat16
@@ -67,9 +65,9 @@
         return pl.ds(pl.multiple_of(b * ROWS, ROWS), ROWS)
 
     barrier = pltpu.get_barrier_semaphore()
-    for o in range(1, 32):
+    for o in range(2, 32, 2):
         pl.semaphore_signal(barrier, inc=1, device_id=(sec, (t + o) % 32), device_id_type=MESH)
-    for dev in (*heirs, (before, t), (before, across)):
+    for dev in (sibling, *heirs, (before, t), (before, across)):
         pl.semaphore_signal(barrier, inc=1, device_id=dev, device_id_type=MESH)
 
     def cols(j):
@@ -95,7 +93,7 @@
 
     stream = resid[...].astype(F32)
     scale = lax.rsqrt(jnp.mean(stream * stream, axis=-1, keepdims=True) + 1e-05)
-    pl.semaphore_wait(barrier, 35)
+    pl.semaphore_wait(barrier, 20)
 
     sends = []
 
@@ -200,8 +198,6 @@
         return lambda: project_kv(j)
 
     actions = [(0, send_weights)]
-    if CARRY < 5:
-        actions.append((CARRY, send_carry))
     for j in range(NC):
         actions += [(j * AG_LAP + when, act) for when, act in ag_actions(j)]
         if j < NC - 1:
@@ -214,7 +210,7 @@
     kv_rows = pl.ds(pl.multiple_of((z // 4) * 128 + yh * 64, 64), 64)
     kv_copies = []
     for n in range(4):
-        zz, yy = 2 * (z % 4) + n // 2, n % 2
+        zz, yy = 2 * (z % 4) + (n // 2 + 1 - z // 4) % 2, (n + 1 + yh) % 2
         mine = (zz == z) & (yy == yh)
         copy = pltpu.make_async_remote_copy(
             src_ref=kvs, dst_ref=kvr.at[c, kv_rows],
@@ -231,22 +227,31 @@
         def _(copy=copy):
             copy.start()
 
-    if CARRY == 5.1:
-        send_carry()
     for j in range(NC - 1):
         project_q(j)
 
     docs = doc_ids[...].astype(F32)
-    row = lax.broadcasted_iota(jnp.int32, (TOK, 1), 0)
-    mine_at = ((row // 16) * 32 + c * 16 + row % 16).astype(F32)
     key = lax.broadcasted_iota(jnp.int32, (1, 2 * TOK), 1)
     key_at = (((key % TOK) // 16) * 32 + (key // TOK) * 16 + key % 16).astype(F32)
-    first = jnp.zeros((TOK, 1), F32)
-    for k in range(1, 4):
-        begin = jnp.sum(jnp.where(docs < k, 1.0, 0.0), axis=-1, keepdims=True)
-        first = jnp.maximum(first, jnp.where(mine_at >= begin, begin, 0.0))
-    mask = (key_at <= mine_at) & (key_at >= first)
-
+    begins = [
+        jnp.sum(jnp.where(docs < k, 1.0, 0.0), axis=-1, keepdims=True) for k in range(1, 4)
+    ]
+
+    def planes(g):
+        return [
+            pl.ds(pl.multiple_of((z + 2 + 4 * g + k) % Z * 32, 32), 32) for k in range(4)
+        ]
+
+    def mask_of(g):
+        row = lax.broadcasted_iota(jnp.int32, (TOK // 2, 1), 0)
+        plane = (z + 2 + 4 * g + row // 32) % Z
+        mine_at = (plane * 64 + row % 32 // 16 * 32 + c * 16 + row % 16).astype(F32)
+        first = jnp.zeros((TOK // 2, 1), F32)
+        for begin in begins:
+            first = jnp.maximum(first, jnp.where(mine_at >= begin, begin, 0.0))
+        return (key_at <= mine_at) & (key_at >= first)
+
+    mask = mask_of(0)
 
     def kv_relay(i, kind, half, targets):
         rows = pl.ds(kind * 128 + half * 64, 64)
@@ -264,13 +269,10 @@
             copy.start()
             sends.append(copy)
 
-    if CARRY == 5.12:
-        send_carry()
+    send_carry()
     project_q(NC - 1)
     for i in KV_ORDER:
         kv_relay(i, i // 2, i % 2, [(sibling, 4 + i)])
-    if CARRY == 5.15:
-        send_carry()
     for i in range(4):
         rows = pl.ds(i * 64, 64)
         ref = kvr.at[1 - c, rows]
@@ -279,20 +281,30 @@
             device_id=sibling, device_id_type=MESH,
         ).wait_recv()
 
-    if CARRY == 5.2:
-        send_carry()
     keys = jnp.concatenate([kvr[0, :128, :], kvr[1, :128, :]], axis=1)
     values = jnp.concatenate([kvr[0, 128:, :], kvr[1, 128:, :]], axis=1)
-    for h in range(4):
-        query = accq[:, h * HD : (h + 1) * HD].astype(BF16)
-        scores = jnp.dot(query, keys, preferred_element_type=F32) * HD**-0.5
-        scores = jnp.where(mask, scores, -1e30)
-        top = jnp.max(scores, axis=-1, keepdims=True)
-        weight = jnp.exp(scores - top)
-        probs = (weight * (1.0 / jnp.sum(weight, axis=-1, keepdims=True))).astype(BF16)
-        ctx[:, h * HD : (h + 1) * HD] = lax.dot_general(
-            probs, values, (((1,), (1,)), ((), ())), preferred_element_type=F32
-        ).astype(BF16)
+    def attend(g, mask):
+        for h in range(4):
+            span = slice(h * HD, (h + 1) * HD)
+            query = jnp.concatenate([accq[rows, span] for rows in planes(g)], axis=0).astype(BF16)
+            scores = jnp.dot(query, keys, preferred_element_type=F32) * HD**-0.5
+            scores = jnp.where(mask, scores, -1e30)
+            top = jnp.max(scores, axis=-1, keepdims=True)
+            weight = jnp.exp(scores - top)
+            probs = (weight * (1.0 / jnp.sum(weight, axis=-1, keepdims=True))).astype(BF16)
+            ctx[g, :, span] = lax.dot_general(
+                probs, values, (((1,), (1,)), ((), ())), preferred_element_type=F32
+            ).astype(BF16)
+
+    def out_project(j, g):
+        for n in range(0, KC, 512):
+            term = jnp.dot(
+                ctx[g], wo[:, j * KC + n : j * KC + n + 512], preferred_element_type=F32
+            ).astype(BF16)
+            for k, rows in enumerate(planes(g)):
+                part[j, rows, n : n + 512] = term[k * 32 : (k + 1) * 32]
+
+    attend(0, mask)
 
     sent = [0] * NC
 
@@ -336,10 +348,7 @@
 
         def begin():
             weight_ready(1 + NC + j)
-            for n in range(0, KC, 512):
-                part[j, :, n : n + 512] = jnp.dot(
-                    ctx[...], wo[:, j * KC + n : j * KC + n + 512], preferred_element_type=F32
-                ).astype(BF16)
+            out_project(j, 0)
             rs_send(j, OTHER, 4, YY, YE[4])
             rs_send(j, OTHER, -3 * e, back, QB[2])
 
@@ -363,6 +372,7 @@
         return [
             (0, begin),
             (RS_Y[0], cross(3)),
+            (RS_Y[0] + 0.06, lambda: out_project(j, 1)),
             (RS_Y[1], cross(2)),
             (RS_Y[2], cross(1)),
             (T_B[0], lambda: rs_send(j, SAME, -3 * e, back, RB[2])),
@@ -378,9 +388,7 @@
             (5, finish(SAME, [RF[0], RB[0]])),
         ]
 
-    actions = []
-    if CARRY >= 6:
-        actions.append((CARRY - 6, send_carry))
+    actions = [(RS_Y[0] + 0.05, lambda: attend(1, mask_of(1)))]
     for j in range(NC):
         actions += [(j * RS_LAP + when, act) for when, act in rs_actions(j)]
     for _, act in sorted(actions, key=lambda item: item[0]):
@@ -436,7 +444,7 @@
             pltpu.VMEM((64, TOK), F32),
             pltpu.VMEM((64, TOK), BF16),
             pltpu.VMEM((2, 256, TOK), BF16),
-            pltpu.VMEM((TOK, 512), BF16),
+            pltpu.VMEM((2, TOK // 2, 512), BF16),
             pltpu.VMEM((NC, TOK, KC), BF16),
             pltpu.VMEM((NC, SLOTS, ROWS, KC), BF16),
             pltpu.VMEM((ROWS, D), BF16),
@@ -462,8 +470,6 @@
         resid[0], pending[0], doc_ids, norm_gain,
         q_weight[0], kv_weight[0].T, o_weight[0],
     )
-    if FINISH == 0:
-        return carried[None], (sums[0].astype(F32) + sums[1].astype(F32)).astype(BF16)[None]
     out = jax.ShapeDtypeStruct((ROWS, D), BF16)
     next_resid, next_output = pl.pallas_call(
         finish_kernel,

time: 102 us -> 100 us (0.980)
  Pallas kernels: 99.7 us -> 98.6 us
    pallas_call x1, Pallas kernels: 97.7 us -> 96.7 us  [body(): pl.pallas_call(kernel, out_shape=(jax.ShapeDtypeStruct((ROWS, D), BF16),...]
where the time goes in v5:
time: 100 us; the launch traced here: 99.3 us
  Pallas kernels  98.6 us (99%)
    pallas_call x1, Pallas kernels, body(): pl.pallas_call(kernel, out_shape=(jax.ShapeDtypeStruct((ROWS, D), BF16),...  96.7 us

profile of v5, /device:TPU:32, one launch (start us, length us, event | category | flops | bytes accessed | tf_op | source)
XLA Modules:
  0.0 99.3 jit_solution(18286817451041163736)
XLA Ops:
  0.6 96.7 %module.1 = (bf16[16,8192]{1,0:T(8,128)(2,1)}, bf16[2,16,8192]{2,1,0:T(8,128)(2,1)}) custom-call(bf16[16,8192]{1,0:T(8,128)(2,1)} %bitcast.12, bf16[16,8192]{1,0:T(8,128)(2,1)} %bitcast.13, s32[1,512]{1,0:T(1,128)} %doc_ids.1, bf16[1,8192]{1,0:T(2,128)(2,1)} %gain.1, bf16[8192,256]{1,0:T(8,128)(2,1)} %bitcast.9, bf16[32,8192]{1,0:T(8,128)(2,1)} %bitcast.11, ...), custom_call_target="tpu_custom_call" | custom-call | tf_op jit(solution)/shard_map/module/pallas_call | solution.py:430
  97.3 1.9 %finish.1 = (bf16[16,8192]{1,0:T(8,128)(2,1)}, bf16[16,8192]{1,0:T(8,128)(2,1)}) custom-call(bf16[16,8192]{1,0:T(8,128)(2,1)} %get-tuple-element.6.carried, bf16[2,16,8192]{2,1,0:T(8,128)(2,1)} %get-tuple-element.7.sums), custom_call_target="tpu_custom_call" | custom-call | tf_op jit(solution)/shard_map/finish/pallas_call | solution.py:474

commit v6 on v5

--- a/solution.py
+++ b/solution.py
@@ -23,6 +23,7 @@
 AG_MM = 0.5
 RS_LAP = 0
 RS_Q = 2.5
+FIN_LAG = 1.5
 RS_Y = (0.1, 0.2, 0.3)
 MESH = pl.DeviceIdType.MESH
 F32 = jnp.float32
@@ -384,8 +385,8 @@
             (T_B[2], relay(SAME, -e, [RB[1]], back, RB[0])),
             (T_F[2], relay(SAME, 2 * e, [YE[2], RF[2]], fore, RF[1])),
             (RS_Q, finish(OTHER, [QB[0]])),
-            (T_F[3], relay(SAME, e, [YE[1], RF[1]], fore, RF[0])),
-            (5, finish(SAME, [RF[0], RB[0]])),
+            (T_F[3] + j / 100, relay(SAME, e, [YE[1], RF[1]], fore, RF[0])),
+            (T_F[3] + (j + FIN_LAG) / 100, finish(SAME, [RF[0], RB[0]])),
         ]
 
     actions = [(RS_Y[0] + 0.05, lambda: attend(1, mask_of(1)))]

time: 100 us -> 100 us (level)
  no operation moved by 1% of the time
where the time goes in v6:
time: 100 us; the launch traced here: 99 us
  Pallas kernels  98.3 us (98%)
    pallas_call x1, Pallas kernels, body(): pl.pallas_call(kernel, out_shape=(jax.ShapeDtypeStruct((ROWS, D), BF16),...  96.4 us

profile of v6, /device:TPU:32, one launch (start us, length us, event | category | flops | bytes accessed | tf_op | source)
XLA Modules:
  0.0 99.0 jit_solution(9265749340457970052)
XLA Ops:
  0.6 96.4 %module.1 = (bf16[16,8192]{1,0:T(8,128)(2,1)}, bf16[2,16,8192]{2,1,0:T(8,128)(2,1)}) custom-call(bf16[16,8192]{1,0:T(8,128)(2,1)} %bitcast.12, bf16[16,8192]{1,0:T(8,128)(2,1)} %bitcast.13, s32[1,512]{1,0:T(1,128)} %doc_ids.1, bf16[1,8192]{1,0:T(2,128)(2,1)} %gain.1, bf16[8192,256]{1,0:T(8,128)(2,1)} %bitcast.9, bf16[32,8192]{1,0:T(8,128)(2,1)} %bitcast.11, ...), custom_call_target="tpu_custom_call" | custom-call | tf_op jit(solution)/shard_map/module/pallas_call | solution.py:431
  97.0 1.9 %finish.1 = (bf16[16,8192]{1,0:T(8,128)(2,1)}, bf16[16,8192]{1,0:T(8,128)(2,1)}) custom-call(bf16[16,8192]{1,0:T(8,128)(2,1)} %get-tuple-element.6.carried, bf16[2,16,8192]{2,1,0:T(8,128)(2,1)} %get-tuple-element.7.sums), custom_call_target="tpu_custom_call" | custom-call | tf_op jit(solution)/shard_map/finish/pallas_call | solution.py:475
